TPU v7x, 256 devices: a whole 4x4x8 slice. The times are simulated.
256 devices in a mesh: dp: 4 (over x), graph: 64 (over z, y, core).
Axes of the slice: x: 4, y: 4, z: 8, core: 2. Of those that a mesh axis runs over, the one named last changes fastest.
Arguments:
- tokens: bfloat16 [8192, 32, 768], P(('dp', 'graph'))
- w_in: bfloat16 [768, 3072], replicated, may hold values from -0.21875 to 0.21875
- w_out: bfloat16 [3072, 768], replicated, may hold values from -0.109375 to 0.109375
- tile_weights: bfloat16 [8192, 128, 128], P(('dp', 'graph')), may hold values from 0 to 18, as said below
- tile_src: int32 [8192], P(('dp', 'graph')), may hold values from 0 to 15
- tile_dst: int32 [8192], P(('dp', 'graph')), may hold values from 0 to 15, as said below
- w_sage: bfloat16 [1536, 1024], P(None, 'dp'), may hold values from -0.15625 to 0.15625
Outputs:
- embeddings: bfloat16 [8192, 768], P(('dp', 'graph'))
- node_states: bfloat16 [8192, 1024], P(('dp', 'graph'))
Inputs may be any that keep to these rules, and one draw needn't show every extreme that they name: `tile_weights`: zero where a tile has no edge, positive on an edge. `tile_dst`: among the 32 tiles of one device no destination block appears more than 4 times; in every slab one block, drawn from the seed, is the destination of exactly 4 tiles of every device of the slab.
All inputs are finite; a program needn't handle non-finite values.
Results may differ from a plain program's by a relative error of at most 0.0042.
The roundings to bfloat16 on the way count: a program that leaves them out, or rounds other values in their place, can miss the bound.
Values may be sent and summed in bfloat16 or wider, within the bound.
A program may use at most 128 MiB of HBM per device.

v0:
```python
import jax
import jax.numpy as jnp
from jax import lax
from jax.sharding import PartitionSpec as P

BLK = 128


EPS = 1e-05


def encode(block_tokens, w_in, w_out):
    node_total, token_total, feature_width = block_tokens.shape
    flat = block_tokens.reshape(node_total * token_total, feature_width)
    hidden = jax.nn.gelu(
        jnp.dot(flat, w_in, preferred_element_type=jnp.float32), approximate=False
    ).astype(jnp.bfloat16)
    mixed = flat.astype(jnp.float32) + jnp.dot(hidden, w_out, preferred_element_type=jnp.float32)
    center = mixed - jnp.mean(mixed, axis=1, keepdims=True)
    normed = center * lax.rsqrt(jnp.mean(center * center, axis=1, keepdims=True) + EPS)
    return jnp.mean(normed.reshape(node_total, token_total, feature_width), axis=1).astype(
        jnp.bfloat16
    )


def on_device(tokens, w_in, w_out, tile_weights, tile_src, tile_dst, w_sage):
    embedded = encode(tokens, w_in, w_out)
    feature_width = embedded.shape[1]
    slab_emb = lax.all_gather(embedded, "graph", axis=0, tiled=True)
    slab_nodes = slab_emb.shape[0]
    blocks = slab_nodes // BLK
    block_ids = jnp.arange(blocks, dtype=jnp.int32)
    block_match = (tile_dst[:, None] == block_ids[None, :]).astype(jnp.int32)
    source_rows = jnp.take(slab_emb.reshape(blocks, BLK, feature_width), tile_src, axis=0)
    messages = jnp.einsum(
        "tij,tjc->tic", tile_weights, source_rows, preferred_element_type=jnp.float32
    )
    weight_sums = jnp.sum(tile_weights, axis=2, dtype=jnp.float32)
    dest_table = block_match.astype(jnp.float32)
    partial_value = jnp.einsum("tb,tic->bic", dest_table, messages, precision=lax.Precision.HIGHEST)
    degree_part = jnp.einsum("tb,ti->bi", dest_table, weight_sums, precision=lax.Precision.HIGHEST)
    neighbor_sums, degree = (
        lax.psum_scatter(
            partial_value.reshape(slab_nodes, feature_width),
            "graph",
            scatter_dimension=0,
            tiled=True,
        ),
        lax.psum_scatter(degree_part.reshape(slab_nodes), "graph", scatter_dimension=0, tiled=True),
    )
    aggregated = (neighbor_sums * lax.rsqrt(1.0 + degree)[:, None]).astype(jnp.bfloat16)
    joined = jnp.concatenate([embedded, aggregated], axis=1)
    preact = jnp.dot(
        joined, lax.all_gather(w_sage, "dp", axis=1, tiled=True), preferred_element_type=jnp.float32
    )
    activated = jnp.maximum(preact, 0.0)
    node_out = activated * lax.rsqrt(jnp.mean(activated * activated, axis=1, keepdims=True) + EPS)
    return (embedded, node_out.astype(jnp.bfloat16))


def solution(mesh):
    return jax.shard_map(
        on_device,
        mesh=mesh,
        in_specs=(
            P(("dp", "graph"), None, None),
            P(),
            P(),
            P(("dp", "graph"), None, None),
            P(("dp", "graph")),
            P(("dp", "graph")),
            P(None, "dp"),
        ),
        out_specs=(P(("dp", "graph"), None), P(("dp", "graph"), None)),
        check_vma=False,
    )
```

profile of v0, /device:TPU:1, one launch (start us, length us, event | category | flops | bytes accessed | tf_op | source)
XLA Modules:
  0.0 325.2 jit_solution(7237322756730343878)
XLA Ops:
  8.0 0.0 all-gather.3.cloned.1.call-start
  8.1 37.9 %fusion.67 = (f32[1024]{0:T(1024)S(1)}, f32[1024,768]{1,0:T(8,128)S(1)}) fusion(bf16[3072,768]{1,0:T(8,128)(2,1)} %param.9, bf16[1024,768]{1,0:T(8,128)(2,1)} %bitcast.22, bf16[768,3072]{1,0:T(8,128)(2,1)} %param.8), kind=kOutput, calls=%fused_computation.90 | convolution fusion | flops 9870507008 | bytes 14159872 | tf_op jit(solution)/shard_map/dot_general | solution.py:18
  46.0 0.5 multiply_reduce_fusion
  46.5 0.7 bitcast_reduce_fusion
  47.2 0.6 multiply_convert_fusion.2
  47.8 0.0 all-gather.3.cloned.1.call-update
  47.9 0.0 reduce-scatter.2.cloned.1.call-start
  48.0 82.6 %all-gather.3.cloned.1.call-done = bf16[2048,768]{1,0:T(8,128)(2,1)} async-done(((bf16[32,768]{1,0:T(8,128)(2,1)}), bf16[2048,768]{1,0:T(8,128)(2,1)}) %all-gather.3.cloned.1.call-update) | async-done | bytes 3145744 | tf_op jit(solution)/shard_map/all_gather | solution.py:29
  130.5 5.4 %gather_fusion = bf16[32,128,768]{2,1,0:T(8,128)(2,1)} fusion(bf16[16,128,768]{2,1,0:T(8,128)(2,1)} %bitcast.21, s32[1024]{0:T(1024)S(1)} %pad_clamp_fusion), kind=kCustom, calls=%fused_computation | custom fusion | bytes 12583040 | tf_op jit(solution)/shard_map/jit(_take)/gather | solution.py:34
  136.0 9.3 %fusion.15 = f32[32,128,768]{1,2,0:T(8,128)} fusion(bf16[32,128,128]{2,1,0:T(8,128)(2,1)S(1)} %copy-done, bf16[32,128,768]{2,1,0:T(8,128)(2,1)} %gather_fusion, pred[32]{0:T(512)(128)(4,1)S(1)} %compare_and_fusion), kind=kOutput, calls=%fused_computation.24 | convolution fusion | flops 808452096 | bytes 19922976 | tf_op jit(solution)/shard_map/tij,tjc->tic/dot_general | solution.py:35
  145.3 12.9 %copy.13 = f32[32,128,768]{2,0,1:T(8,128)} copy(f32[32,128,768]{1,2,0:T(8,128)} %fusion.15) | data formatting | bytes 25165824 | tf_op jit(solution)/shard_map/tij,tjc->tic/dot_general | solution.py:35
  158.2 8.7 %fusion.26 = f32[16,128,768]{2,0,1:T(8,128)S(1)} fusion(f32[32,128,768]{2,0,1:T(8,128)} %copy.13, s32[32]{0:T(128)S(1)} %copy-done.2), kind=kOutput, calls=%fused_computation.41 | convolution fusion | flops 603981312 | bytes 18874496 | tf_op jit(solution)/shard_map/tb,tic->bic/dot_general | solution.py:40
  167.0 6.3 %copy.14 = f32[16,128,768]{2,1,0:T(8,128)} copy(f32[16,128,768]{2,0,1:T(8,128)S(1)} %fusion.26) | data formatting | bytes 12582912 | tf_op jit(solution)/shard_map/tb,tic->bic/dot_general | solution.py:40
  173.3 0.0 all-gather.5.cloned.1.call-start
  173.3 0.5 all-gather.5.cloned.1.call-update
  173.9 0.6 dynamic-slice
  175.1 0.3 convert_reduce_fusion
  175.5 0.1 convolution_bitcast_fusion
  175.6 126.1 %all-reduce = f32[2048]{0:T(1024)S(1)} all-reduce(f32[2048]{0:T(1024)S(1)} %convolution_bitcast_fusion), channel_id=3, replica_groups=mesh['dp'=4,'graph'=64] {'graph'}, use_global_device_ids=true, to_apply=%region_5.6.clone | all-reduce | flops 2048 | bytes 16384
  301.7 0.1 fusion.34
  301.8 11.6 %reduce-scatter.2.cloned.1.call-done = f32[32,768]{1,0:T(8,128)} async-done(((f32[2048,768]{1,0:T(8,128)}), f32[32,768]{1,0:T(8,128)}) %reduce-scatter.2.cloned.1.call-update) | async-done | bytes 98320 | tf_op jit(solution)/shard_map/reduce_scatter | solution.py:43
  313.4 1.0 multiply_convert_fusion.1
  314.4 2.6 multiply_reduce_fusion.1
  317.1 0.7 multiply_convert_fusion
  (18 shorter events, 0.1 us)
Async XLA Ops:
  8.0 122.5 %all-gather.3.cloned.1.call-start = ((), (), s32[]{:S(2)}) async-start(), calls=%async_computation.1 | async-start | bytes 3194880 | tf_op jit(solution)/shard_map/all_gather | solution.py:29
  8.0 39.9 %copy-start.3 = (s32[32]{0:T(128)S(1)}, s32[32]{0:T(128)}, u32[]{:S(2)}) copy-start(s32[32]{0:T(128)} %param.11) | copy-start | bytes 388
  47.2 88.8 %copy-start = (bf16[32,128,128]{2,1,0:T(8,128)(2,1)S(1)}, bf16[32,128,128]{2,1,0:T(8,128)(2,1)}, u32[]{:S(2)}) copy-start(bf16[32,128,128]{2,1,0:T(8,128)(2,1)} %param.10) | copy-start | bytes 3145732
  47.9 265.6 %reduce-scatter.2.cloned.1.call-start = ((), (), s32[]{:S(2)}) async-start(), calls=%async_computation.2 | async-start | bytes 6389760 | tf_op jit(solution)/shard_map/reduce_scatter | solution.py:43
  145.3 12.9 %copy-start.2 = (s32[32]{0:T(128)S(1)}, s32[32]{0:T(128)}, u32[]{:S(2)}) copy-start(s32[32]{0:T(128)} %param.12) | copy-start | bytes 388
  166.9 6.9 %copy-start.4 = (u32[256]{0:T(256)S(1)}, u32[256]{0:T(256)}, u32[]{:S(2)}) copy-start(u32[256]{0:T(256)} %constant.98) | copy-start | bytes 3076
  167.0 147.4 %copy-start.1 = (bf16[32,768]{1,0:T(8,128)(2,1)S(1)}, bf16[32,768]{1,0:T(8,128)(2,1)}, u32[]{:S(2)}) copy-start(bf16[32,768]{1,0:T(8,128)(2,1)} %multiply_convert_fusion.2) | copy-start | bytes 147460
  173.3 141.1 %all-gather.5.cloned.1.call-start = ((), (), s32[]{:S(2)}) async-start(), calls=%async_computation.3 | async-start | bytes 3932160 | tf_op jit(solution)/shard_map/all_gather | solution.py:54
Sparse Core Ops, SparseCore 0:
  48.0 82.5 all-gather.2
  173.4 139.9 reduce-scatter.1
Sparse Core Ops, SparseCore 1:
  175.6 41.2 all-gather.4
where the time goes:
time: 330 us; the launch traced here: 325 us
  blocking collectives  126 us (38%)
  waiting for transfers between devices  94.8 us (29%)
  matrix products  58.7 us (18%)
  local copies, waits for them, and re-layouts  25.3 us (8%)
  between operations  16.3 us (5%)
  other arithmetic  3.95 us (1%)
    unnamed x1, blocking collectives  126 us
    all_gather x1, waiting for transfers between devices, on_device(): slab_emb = lax.all_gather(embedded, 'graph', axis=0, tiled=True)  82.6 us
    dot_general x1, matrix products, encode(): jnp.dot(hidden, w_out, preferred_element_type=jnp.float32)  37.9 us
    dot_general x1, local copies, waits for them, and re-layouts, on_device(): jnp.einsum('tij,tjc->tic', tile_weights, source_rows, preferred_element_t...  12.9 us
    reduce_scatter x1, waiting for transfers between devices, on_device(): lax.psum_scatter(partial_value.reshape(slab_nodes, feature_width), 'graph...  11.6 us
    dot_general x1, matrix products, on_device(): jnp.einsum('tij,tjc->tic', tile_weights, source_rows, preferred_element_t...  9.3 us
    dot_general x1, matrix products, on_device(): jnp.einsum('tb,tic->bic', dest_table, messages, precision=lax.Precision.H...  8.74 us
  transfers between devices with their start and end apart: 3, of which 2 were waited for; matrix products, arithmetic and copies ran while one was open for 1% of the time, Pallas kernels for 0%

commit v1 on v0

v1 whole, which is shorter than its diff:
```python
import functools

import jax
import jax.numpy as jnp
from jax import lax
from jax.experimental import pallas as pl
from jax.experimental.pallas import tpu as pltpu
from jax.sharding import PartitionSpec as P

EPS = 1e-05
MESH = pl.DeviceIdType.MESH

NX, NZ, NY, NC = 4, 8, 4, 2
D, FF, HID = 768, 3072, 1024
BLK, TILES, BLOCKS = 128, 32, 16
NODES, TOK = 32, 32
CHUNKS = 4
CN = NODES // CHUNKS
ROWS = CN * TOK
FB = 768
NFB = FF // FB
QUAD = 4
SUB = BLK // QUAD
FC = 256
NFC = D // FC
BF, F32 = jnp.bfloat16, jnp.float32


def kernel(
    tok_ref, win_ref, wout_ref, tw_ref, src_ref, dst_ref, ws_ref,
    emb_out, node_out,
    win, wout, tok, tiles, ids, spread, adj, emb, wg, own, out_y, in_y, out_z, in_z,
    deg, deg_in, deg_sum, deg_all,
    load_sem, tile_s, tile_r, id_s, id_r, w_s, w_r, z_s, z_r, y_s, y_r, c_s, c_r,
    vy_s, vy_r, vz_s, vz_r, d_s, d_r,
):
    xi = lax.axis_index("dp")
    g = lax.axis_index("graph")
    z, y, c = g // 8, (g // 2) % 4, g % 2
    q = g % 4
    yh = y // 2

    def at(zz, yy, cc):
        return (xi, (zz * NY + yy) * NC + cc)

    def zoff(j):
        return lax.rem(z + j + NZ, NZ)

    def yoff(j):
        return lax.rem(y + j + NY, NY)

    def xoff(j):
        return lax.rem(xi + j + NX, NX)

    def remote(src, dst, ss, rs, dev):
        return pltpu.make_async_remote_copy(
            src_ref=src, dst_ref=dst, send_sem=ss, recv_sem=rs, device_id=dev, device_id_type=MESH
        )

    sib = at(z, y, 1 - c)
    def load_tok(k):
        return pltpu.make_async_copy(tok_ref.at[pl.ds(k * CN, CN)], tok.at[pl.ds(k * CN, CN)], load_sem.at[k])

    def load_in(j):
        cols = pl.ds(j * FB, FB)
        return pltpu.make_async_copy(win_ref.at[:, cols], win.at[:, cols], load_sem.at[4 + j])

    def load_out(j):
        rows = pl.ds(j * FB, FB)
        return pltpu.make_async_copy(wout_ref.at[rows], wout.at[rows], load_sem.at[8 + j])

    def load_tiles():
        return pltpu.make_async_copy(
            tw_ref.at[:, pl.ds(pl.multiple_of(q * SUB, SUB), SUB)], tiles.at[q], load_sem.at[12]
        )

    def load_ws(h):
        return pltpu.make_async_copy(ws_ref.at[pl.ds(h * D, D)], wg.at[h, xi], load_sem.at[13 + h])

    peers = [at(zoff(j), y, c) for j in range(1, NZ)]
    peers += [at(z, yoff(j), c) for j in range(1, NY)]
    ypair = y + 1 - 2 * (y % 2)
    peers += [sib, at(z, ypair, 1 - c), (xoff(1), g), (xoff(-1), g)]
    barrier = pltpu.get_barrier_semaphore()
    for dev in peers:
        pl.semaphore_signal(barrier, inc=1, device_id=dev, device_id_type=MESH)

    load_tok(0).start()
    for j in range(NFB):
        load_in(j).start()
        load_out(j).start()
    for k in range(1, CHUNKS):
        load_tok(k).start()
    load_tiles().start()
    for h in range(2):
        load_ws(h).start()

    lane = lax.broadcasted_iota(jnp.int32, (8, 128), 1) - q * TILES
    mine = jnp.full((8, 128), -1, jnp.int32)
    for t in range(TILES):
        mine = jnp.where(lane == t, src_ref[t] * BLOCKS + dst_ref[t], mine)
    ids[q] = mine

    pl.semaphore_wait(barrier, len(peers))

    quad = [(at(z, y, 1 - c), q + 1 - 2 * (q % 2)), (at(z, ypair, c), lax.rem(q + 2, 4)),
            (at(z, ypair, 1 - c), lax.rem(q + 2, 4) + 1 - 2 * (q % 2))]

    def tile_send(n):
        dev, dq = quad[n]
        return remote(tw_ref.at[:, pl.ds(pl.multiple_of(dq * SUB, SUB), SUB)], tiles.at[q],
                      tile_s.at[n], tile_r.at[n], dev)

    def tile_recv(n):
        dev, dq = quad[n]
        return remote(tiles.at[dq], tiles.at[dq], tile_s.at[n], tile_r.at[n], dev)

    def id_send(n):
        return remote(ids.at[q], ids.at[q], id_s.at[n], id_r.at[n], quad[n][0])

    def id_recv(n):
        dq = quad[n][1]
        return remote(ids.at[dq], ids.at[dq], id_s.at[n], id_r.at[n], quad[n][0])

    for n in range(3):
        id_send(n).start()
        tile_send(n).start()

    half = pl.ds(pl.multiple_of(c * D, D), D)

    def w_send(n):
        return remote(ws_ref.at[half], wg.at[c, xi], w_s.at[n], w_r.at[n], (xoff(1 - 2 * n), g))

    def w_recv(n):
        slot = wg.at[c, xoff(2 * n - 1)]
        return remote(slot, slot, w_s.at[n], w_r.at[n], (xoff(1 - 2 * n), g))

    def w_fwd(n):
        rows = pl.ds(n * (D // 2), D // 2)
        slot = wg.at[c, xoff(2 * n - 1), rows]
        return remote(slot, slot, w_s.at[2 + n], w_r.at[2 + n], (xoff(1 - 2 * n), g))

    def w_fwd_recv(n):
        rows = pl.ds(n * (D // 2), D // 2)
        slot = wg.at[c, xoff(2), rows]
        return remote(slot, slot, w_s.at[2 + n], w_r.at[2 + n], (xoff(1 - 2 * n), g))

    def w_sib(n):
        slot = wg.at[c, xoff(n)]
        return remote(slot, slot, w_s.at[3 + n], w_r.at[3 + n], sib)

    def w_sib_recv(n):
        slot = wg.at[1 - c, xoff(n)]
        return remote(slot, slot, w_s.at[3 + n], w_r.at[3 + n], sib)

    for n in range(2):
        w_send(n).start()

    def z_send(k, j):
        slot = emb.at[z, y, c, k]
        return remote(slot, slot, z_s.at[k, j], z_r.at[k, j], at(zoff(j), y, c))

    def z_recv(k, j):
        slot = emb.at[zoff(-j), y, c, k]
        return remote(slot, slot, z_s.at[k, j], z_r.at[k, j], at(zoff(j), y, c))

    def y_send(k, j):
        slot = emb.at[:, y, c, k]
        return remote(slot, slot, y_s.at[k, j], y_r.at[k, j], at(z, yoff(j), c))

    def y_recv(k, j):
        slot = emb.at[:, yoff(-j), c, k]
        return remote(slot, slot, y_s.at[k, j], y_r.at[k, j], at(z, yoff(j), c))

    def c_send(k):
        slot = emb.at[:, :, c, k]
        return remote(slot, slot, c_s.at[k], c_r.at[k], sib)

    def c_recv(k):
        slot = emb.at[:, :, 1 - c, k]
        return remote(slot, slot, c_s.at[k], c_r.at[k], sib)

    def go_z(k):
        for j in (4, 3, 5, 2, 6, 1, 7):
            z_send(k, j).start()

    def go_y(k):
        for j in range(1, NZ):
            z_recv(k, j).wait_recv()
        for j in (2, 1, 3):
            y_send(k, j).start()

    def go_c(k):
        for j in range(1, NY):
            y_recv(k, j).wait_recv()
        c_send(k).start()

    def encode(k, carry):
        load_tok(k).wait()
        x = tok[pl.ds(k * CN, CN)].reshape(ROWS, D)
        acc = x.astype(F32)
        for j in range(NFB):
            @pl.when(k == 0)
            def _():
                load_in(j).wait()
                load_out(j).wait()

            h = jnp.dot(x, win[:, j * FB:(j + 1) * FB], preferred_element_type=F32)
            a = (h * 0.5 * (1.0 + lax.erf(h * 0.7071067811865476))).astype(BF)
            acc = acc + jnp.dot(a, wout[j * FB:(j + 1) * FB, :], preferred_element_type=F32)
            if j == 1:
                @pl.when(k >= 2)
                def _():
                    go_y(k - 2)

                @pl.when(k == 3)
                def _():
                    go_c(0)
                    for n in range(2):
                        w_recv(n).wait_recv()
                        w_fwd(n).start()
        cent = acc - jnp.mean(acc, axis=1, keepdims=True)
        var = jnp.mean(cent * cent, axis=1, keepdims=True)
        norm = cent * lax.rsqrt(var + EPS)
        emb[z, y, c, k] = jnp.mean(norm.reshape(CN, TOK, D), axis=1).astype(BF)
        go_z(k)
        return carry

    lax.fori_loop(0, CHUNKS, encode, 0)
    go_y(2)
    go_c(1)
    for n in range(2):
        w_fwd_recv(n).wait_recv()
    for n in range(1, 4):
        w_sib(n).start()

    load_tiles().wait()
    for n in range(3):
        id_recv(n).wait_recv()
        tile_recv(n).wait_recv()
    for n in range(QUAD):
        spread[pl.ds(n * TILES * SUB, TILES * SUB), :] = tiles[n].astype(F32).reshape(TILES * SUB, BLK)
    cell = jnp.max(ids[...], axis=0)[0:1, :]
    pick = (lax.broadcasted_iota(jnp.int32, (BLOCKS * BLOCKS, QUAD * TILES), 0) == cell).astype(BF)
    deg[...] = jnp.zeros_like(deg)
    dlane = lax.broadcasted_iota(jnp.int32, (BLOCKS, BLK), 1)

    def place(i, carry):
        rows = spread[pl.ds(i, QUAD * TILES, stride=SUB), :].astype(BF)
        got = jnp.dot(pick, rows, preferred_element_type=F32)
        total = got[:BLOCKS]
        for s in range(BLOCKS):
            part = got[s * BLOCKS:(s + 1) * BLOCKS]
            if s:
                total = total + part
            adj[s, pl.ds(i, BLOCKS, stride=SUB), :] = part
        deg[...] += jnp.where(dlane == i, jnp.sum(total, axis=1, keepdims=True), 0.0)
        return carry

    lax.fori_loop(0, SUB // 2, place, 0)
    go_y(3)
    go_c(2)
    lax.fori_loop(SUB // 2, SUB, place, 0)

    partner = at(z, yoff(2), c)
    d_first = remote(deg, deg_in, d_s.at[0], d_r.at[0], partner)
    d_first.start()
    mine_emb = emb[z, y, c].astype(F32).reshape(NODES, D).astype(BF)
    emb_out[...] = mine_emb
    for h in range(2):
        load_ws(h).wait()
    for n in range(1, 4):
        w_sib_recv(n).wait_recv()
    pre = [jnp.dot(mine_emb, wg[0, n], preferred_element_type=F32) for n in range(NX)]
    d_first.wait_recv()
    deg_sum[...] = deg[...] + deg_in[...]

    def d_send(j):
        return remote(deg_sum, deg_all.at[j], d_s.at[j], d_r.at[j], at(zoff(j), y, c))

    for j in range(1, NZ):
        d_send(j).start()

    go_c(3)
    for k in range(CHUNKS):
        c_recv(k).wait_recv()

    def vy(f):
        return remote(out_y.at[f, :, 1 - yh], in_y.at[f], vy_s.at[f], vy_r.at[f], partner)

    def vz(f, j):
        return remote(out_z.at[f, zoff(j)], in_z.at[f, j], vz_s.at[f, j], vz_r.at[f, j], at(zoff(j), y, c))

    def go_vz(f):
        vy(f).wait_recv()
        both = own[f, :, yh] + in_y[f].astype(F32)
        own[f, :, yh] = both
        out_z[f] = both.astype(BF)
        for j in (4, 3, 5, 2, 6, 1, 7):
            vz(f, j).start()

    a = jnp.concatenate([adj[s].astype(BF) for s in range(BLOCKS)], axis=1)
    for f in range(NFC):
        e = emb[:, :, :, :, :, f * FC:(f + 1) * FC].astype(F32).reshape(NZ * NY * NC * NODES, FC).astype(BF)
        v = jnp.dot(a, e, preferred_element_type=F32).reshape(NZ, 2, SUB, FC)
        own[f] = v
        out_y[f] = v.astype(BF)
        vy(f).start()
        if f:
            go_vz(f - 1)
    go_vz(NFC - 1)

    degree = deg_sum[...]
    for j in range(1, NZ):
        d_send(j).wait_recv()
        degree = degree + deg_all[j]
    block = g // 4
    degree = jnp.sum(
        jnp.where(lax.broadcasted_iota(jnp.int32, (BLOCKS, BLK), 0) == block, degree, 0.0), axis=0, keepdims=True
    )
    on = lax.broadcasted_iota(jnp.int32, (NODES, BLK), 0) == lax.broadcasted_iota(jnp.int32, (NODES, BLK), 1)
    column = jnp.sum(jnp.where(on, jnp.broadcast_to(degree, (NODES, BLK)), 0.0), axis=1, keepdims=True)
    scale = lax.rsqrt(1.0 + column)

    for f in range(NFC):
        total = own[f, z, yh]
        for j in range(1, NZ):
            vz(f, j).wait_recv()
            total = total + in_z[f, j].astype(F32)
        agg = (total * scale).astype(BF)
        for n in range(NX):
            pre[n] = pre[n] + jnp.dot(agg, wg[1, n, f * FC:(f + 1) * FC, :], preferred_element_type=F32)
    act = [jnp.maximum(p, 0.0) for p in pre]
    square = sum(jnp.sum(r * r, axis=1, keepdims=True) for r in act)
    inv = lax.rsqrt(square * (1.0 / HID) + EPS)
    for n in range(NX):
        node_out[:, n * 256:(n + 1) * 256] = (act[n] * inv).astype(BF)

    for n in range(3):
        id_send(n).wait_send()
        tile_send(n).wait_send()
    for n in range(2):
        w_send(n).wait_send()
        w_fwd(n).wait_send()
    for n in range(1, 4):
        w_sib(n).wait_send()
    for k in range(CHUNKS):
        for j in range(1, NZ):
            z_send(k, j).wait_send()
        for j in range(1, NY):
            y_send(k, j).wait_send()
        c_send(k).wait_send()
    d_first.wait_send()
    for j in range(1, NZ):
        d_send(j).wait_send()
    for f in range(NFC):
        vy(f).wait_send()
        for j in range(1, NZ):
            vz(f, j).wait_send()


def on_device(tokens, w_in, w_out, tile_weights, tile_src, tile_dst, w_sage):
    dma = pltpu.SemaphoreType.DMA
    anywhere = pl.BlockSpec(memory_space=pl.ANY)
    smem = pl.BlockSpec(memory_space=pltpu.SMEM)
    vmem = pl.BlockSpec(memory_space=pltpu.VMEM)
    return pl.pallas_call(
        kernel,
        out_shape=(
            jax.ShapeDtypeStruct((NODES, D), BF),
            jax.ShapeDtypeStruct((NODES, HID), BF),
        ),
        in_specs=[anywhere, anywhere, anywhere, anywhere, smem, smem, anywhere],
        out_specs=(vmem, vmem),
        scratch_shapes=[
            pltpu.VMEM((D, FF), BF),
            pltpu.VMEM((FF, D), BF),
            pltpu.VMEM((NODES, TOK, D), BF),
            pltpu.VMEM((QUAD, TILES, SUB, BLK), BF),
            pltpu.VMEM((QUAD, 8, 128), jnp.int32),
            pltpu.VMEM((QUAD * TILES * SUB, BLK), F32),
            pltpu.VMEM((BLOCKS, BLOCKS * SUB, BLK), F32),
            pltpu.VMEM((NZ, NY, NC, CHUNKS, CN, D), BF),
            pltpu.VMEM((2, NX, D, 256), BF),
            pltpu.VMEM((NFC, NZ, 2, SUB, FC), F32),
            pltpu.VMEM((NFC, NZ, 2, SUB, FC), BF),
            pltpu.VMEM((NFC, NZ, SUB, FC), BF),
            pltpu.VMEM((NFC, NZ, SUB, FC), BF),
            pltpu.VMEM((NFC, NZ, SUB, FC), BF),
            pltpu.VMEM((BLOCKS, BLK), F32),
            pltpu.VMEM((BLOCKS, BLK), F32),
            pltpu.VMEM((BLOCKS, BLK), F32),
            pltpu.VMEM((NZ, BLOCKS, BLK), F32),
            dma((15,)),
            dma((3,)), dma((3,)),
            dma((3,)), dma((3,)),
            dma((7,)), dma((7,)),
            dma((CHUNKS, NZ)), dma((CHUNKS, NZ)),
            dma((CHUNKS, NY)), dma((CHUNKS, NY)),
            dma((CHUNKS,)), dma((CHUNKS,)),
            dma((NFC,)), dma((NFC,)),
            dma((NFC, NZ)), dma((NFC, NZ)),
            dma((NZ,)), dma((NZ,)),
        ],
        compiler_params=pltpu.CompilerParams(
            collective_id=0, has_side_effects=True, vmem_limit_bytes=58 * 2**20
        ),
        cost_estimate=pl.CostEstimate(flops=12_000_000_000, bytes_accessed=16_000_000, transcendentals=3_200_000),
        name="encode_and_aggregate",
    )(tokens, w_in, w_out, tile_weights, tile_src, tile_dst, w_sage)


def solution(mesh):
    return jax.shard_map(
        on_device,
        mesh=mesh,
        in_specs=(
            P(("dp", "graph"), None, None),
            P(),
            P(),
            P(("dp", "graph"), None, None),
            P(("dp", "graph")),
            P(("dp", "graph")),
            P(None, "dp"),
        ),
        out_specs=(P(("dp", "graph"), None), P(("dp", "graph"), None)),
        check_vma=False,
    )
```

time: 330 us -> 76.6 us (0.23); the launches traced: 325 us -> 76.4 us
  blocking collectives: 126 us -> 0 us
  waiting for transfers between devices: 94.8 us -> 0 us
  Pallas kernels: 0 us -> 72.9 us
  matrix products: 58.7 us -> 0 us
  local copies, waits for them, and re-layouts: 25.3 us -> 2.89 us
  between operations: 16.3 us -> 0.64 us
  other arithmetic: 3.95 us -> 0 us
    unnamed x1 -> x0, blocking collectives: 126 us -> none
    all_gather x2 -> x0, waiting for transfers between devices: 82.6 us -> none  [the longest x1 82.6 us: on_device(): slab_emb = lax.all_gather(embedded, 'graph', axis=0, tiled=True)]
    pallas_call x0 -> x1, Pallas kernels: none -> 72.9 us  [on_device(): pl.pallas_call(kernel, out_shape=(jax.ShapeDtypeStruct((NODES, D), BF), j...]
    dot_general x5 -> x0, matrix products: 58.7 us -> none  [the longest x1 37.9 us: encode(): jnp.dot(hidden, w_out, preferred_element_type=jnp.float32)]
    dot_general x2 -> x0, local copies, waits for them, and re-layouts: 19.2 us -> none  [the longest x1 12.9 us: on_device(): jnp.einsum('tij,tjc->tic', tile_weights, source_rows, preferred_element_t...]
    reduce_scatter x1 -> x0, waiting for transfers between devices: 11.6 us -> none  [on_device(): lax.psum_scatter(partial_value.reshape(slab_nodes, feature_width), 'graph...]
    gather x1 -> x0, local copies, waits for them, and re-layouts: 5.45 us -> none  [on_device(): jnp.take(slab_emb.reshape(blocks, BLK, feature_width), tile_src, axis=0)]
  transfers between devices with their start and end apart: 3 -> 0, of which waited for: 2 -> 0; matrix products, arithmetic and copies ran while one was open for 1% -> 0% of each run, Pallas kernels for 0% -> 0%
where the time goes in v1:
time: 76.6 us; the launch traced here: 76.4 us
  Pallas kernels  72.9 us (95%)
  local copies, waits for them, and re-layouts  2.89 us (4%)
    pallas_call x1, Pallas kernels, on_device(): pl.pallas_call(kernel, out_shape=(jax.ShapeDtypeStruct((NODES, D), BF), j...  72.9 us
    unnamed x2, local copies, waits for them, and re-layouts  2.89 us

profile of v1, /device:TPU:1, one launch (start us, length us, event | category | flops | bytes accessed | tf_op | source)
XLA Modules:
  0.0 76.4 jit_solution(14982539113227730123)
XLA Ops:
  0.6 72.9 %encode_and_aggregate.1 = (bf16[32,768]{1,0:T(8,128)(2,1)}, bf16[32,1024]{1,0:T(8,128)(2,1)}) custom-call(bf16[32,32,768]{2,1,0:T(8,128)(2,1)} %tok_ref.1, bf16[768,3072]{1,0:T(8,128)(2,1)} %win_ref.1, bf16[3072,768]{1,0:T(8,128)(2,1)} %wout_ref.1, bf16[32,128,128]{2,1,0:T(8,128)(2,1)} %tw_ref.1, s32[32]{0:T(128)} %src_ref.1, s32[32]{0:T(128)} %dst_ref.1, ...), custom_call_target="tpu_custom_call" | custom-call | flops 12000000000 | bytes 16000000 | tf_op jit(solution)/shard_map/encode_and_aggregate/pallas_call | solution.py:367
  73.5 1.4 %copy.11 = bf16[32,768]{1,0:T(8,128)(2,1)} copy(bf16[32,768]{1,0:T(8,128)(2,1)} %get-tuple-element.4) | data formatting | bytes 98304
  75.0 1.5 %copy.12 = bf16[32,1024]{1,0:T(8,128)(2,1)} copy(bf16[32,1024]{1,0:T(8,128)(2,1)} %get-tuple-element.5) | data formatting | bytes 131072

commit v2 on v1

v2 whole, which is shorter than its diff:
```python
import functools

import jax
import jax.numpy as jnp
from jax import lax
from jax.experimental import pallas as pl
from jax.experimental.pallas import tpu as pltpu
from jax.sharding import PartitionSpec as P

EPS = 1e-05
MESH = pl.DeviceIdType.MESH

NX, NZ, NY, NC = 4, 8, 4, 2
D, FF, HID = 768, 3072, 1024
BLK, TILES, BLOCKS = 128, 32, 16
NODES, TOK = 32, 32
CHUNKS = 4
CN = NODES // CHUNKS
ROWS = CN * TOK
FB = 768
NFB = FF // FB
QUAD = 4
SUB = BLK // QUAD
FC = 256
NFC = D // FC
UNROLL = 4
ZORDER = (4, 3, 5, 2, 6, 1, 7)
YORDER = (2, 1, 3)
BF, F32 = jnp.bfloat16, jnp.float32


def kernel(
    tok_ref, win_ref, wout_ref, tw_ref, src_ref, dst_ref, ws_ref,
    emb_out, node_out,
    win, wout, tok, tiles, ids, ids_out, spread, adj, adj_t, emb, wg, own, out_y, in_y, out_z, in_z,
    in_z0, out_p, in_p, emb_v, node_v,
    deg, deg_in, deg_sum, deg_all,
    load_sem, tile_s, tile_r, id_s, id_r, w_s, w_r, ag_s, ag_r,
    vy_s, vy_r, vz_s, vz_r, d_s, d_r,
):
    xi = lax.axis_index("dp")
    g = lax.axis_index("graph")
    z, y, c = g // 8, (g // 2) % 4, g % 2
    q = g % 4
    yh = y // 2

    def at(zz, yy, cc):
        return (xi, (zz * NY + yy) * NC + cc)

    def zoff(j):
        return lax.rem(z + j + NZ, NZ)

    def yoff(j):
        return lax.rem(y + j + NY, NY)

    def xoff(j):
        return lax.rem(xi + j + NX, NX)

    def remote(src, dst, ss, rs, dev):
        return pltpu.make_async_remote_copy(
            src_ref=src, dst_ref=dst, send_sem=ss, recv_sem=rs, device_id=dev, device_id_type=MESH
        )

    sib = at(z, y, 1 - c)
    def load_tok(k):
        return pltpu.make_async_copy(tok_ref.at[pl.ds(k * CN, CN)], tok.at[pl.ds(k * CN, CN)], load_sem.at[k])

    def load_in(j):
        cols = pl.ds(j * FB, FB)
        return pltpu.make_async_copy(win_ref.at[:, cols], win.at[:, cols], load_sem.at[4 + j])

    def load_out(j):
        rows = pl.ds(j * FB, FB)
        return pltpu.make_async_copy(wout_ref.at[rows], wout.at[rows], load_sem.at[8 + j])

    def load_tiles():
        return pltpu.make_async_copy(
            tw_ref.at[:, pl.ds(pl.multiple_of(q * SUB, SUB), SUB)], tiles.at[0], load_sem.at[12]
        )

    def load_ws(h):
        return pltpu.make_async_copy(ws_ref.at[pl.ds(h * D, D)], wg.at[h, xi], load_sem.at[13 + h])

    peers = [at(zoff(j), y, c) for j in range(1, NZ)]
    peers += [at(z, yoff(j), c) for j in range(1, NY)]
    peers += [sib, at(z, yoff(1), 1 - c), at(z, yoff(-1), 1 - c), (xoff(1), g), (xoff(-1), g)]
    barrier = pltpu.get_barrier_semaphore()
    for dev in peers:
        pl.semaphore_signal(barrier, inc=1, device_id=dev, device_id_type=MESH)

    load_tok(0).start()
    for j in range(NFB):
        load_in(j).start()
        load_out(j).start()
    for k in range(1, CHUNKS):
        load_tok(k).start()
    load_tiles().start()
    for h in range(2):
        load_ws(h).start()

    low, high = (0, TILES // 2), (TILES // 2, TILES)
    share = [
        (sib, 1, (0, TILES)),
        (at(z, yoff(1), c), 2, low), (at(z, yoff(-1), c), 2, high),
        (at(z, yoff(1), 1 - c), 3, low), (at(z, yoff(-1), 1 - c), 3, high),
    ]

    lane = lax.broadcasted_iota(jnp.int32, (8, 128), 1)
    mine = jnp.full((8, 128), -1, jnp.int32)
    for t in range(TILES):
        mine = jnp.where(lax.rem(lane, TILES) == t, src_ref[t] * BLOCKS + dst_ref[t], mine)
    for n, (slot, (t0, t1)) in enumerate([(0, (0, TILES))] + [e[1:] for e in share]):
        ids_out[n] = jnp.where((lane >= slot * TILES + t0) & (lane < slot * TILES + t1), mine, -1)

    def tile_send(n):
        dev, slot, (t0, t1) = share[n]
        dq = (1 - c if n in (0, 3, 4) else c) + 2 * ((y % 2) if n == 0 else 1 - y % 2)
        part = pl.ds(t0, t1 - t0)
        return remote(tw_ref.at[part, pl.ds(pl.multiple_of(dq * SUB, SUB), SUB)], tiles.at[slot, part],
                      tile_s.at[0], tile_r.at[0], dev)

    def tile_all():
        slot = tiles.at[pl.ds(1, 3)]
        return remote(slot, slot, tile_s.at[0], tile_r.at[0], sib)

    def id_send(n):
        return remote(ids_out.at[n + 1], ids.at[n], id_s.at[0], id_r.at[0], share[n][0])

    def id_all():
        return remote(ids, ids, id_s.at[0], id_r.at[0], sib)

    half = pl.ds(pl.multiple_of(c * D, D), D)

    def w_send(n):
        return remote(ws_ref.at[half], wg.at[c, xi], w_s.at[n], w_r.at[n], (xoff(1 - 2 * n), g))

    def w_recv(n):
        slot = wg.at[c, xoff(2 * n - 1)]
        return remote(slot, slot, w_s.at[n], w_r.at[n], (xoff(1 - 2 * n), g))

    def w_fwd(n):
        rows = pl.ds(n * (D // 2), D // 2)
        slot = wg.at[c, xoff(2 * n - 1), rows]
        return remote(slot, slot, w_s.at[2 + n], w_r.at[2 + n], (xoff(1 - 2 * n), g))

    def w_fwd_recv(n):
        rows = pl.ds(n * (D // 2), D // 2)
        slot = wg.at[c, xoff(2), rows]
        return remote(slot, slot, w_s.at[2 + n], w_r.at[2 + n], (xoff(1 - 2 * n), g))

    def w_sib(n):
        slot = wg.at[c, xoff(n)]
        return remote(slot, slot, w_s.at[3 + n], w_r.at[3 + n], sib)

    def w_sib_recv(n):
        slot = wg.at[1 - c, xoff(n)]
        return remote(slot, slot, w_s.at[3 + n], w_r.at[3 + n], sib)

    def meet():
        pl.semaphore_wait(barrier, len(peers))
        for n in range(len(share)):
            id_send(n).start()
            tile_send(n).start()
        for n in range(2):
            w_send(n).start()

    def z1(k, j=None):
        slot = emb.at[pl.ds(0, NZ - 1) if j is None else z, y, c, k]
        return remote(slot, slot, ag_s.at[0, k], ag_r.at[0, k], at(zoff(j or 1), y, c))

    def y2(k, j=None):
        slot = emb.at[:, pl.ds(0, NY - 1) if j is None else y, c, k]
        return remote(slot, slot, ag_s.at[1, k], ag_r.at[1, k], at(z, yoff(j or 1), c))

    def c_send(k):
        slot = emb.at[:, :, c, k]
        return remote(slot, slot, ag_s.at[2, k], ag_r.at[2, k], sib)

    def c_recv(k):
        slot = emb.at[:, :, 1 - c, k]
        return remote(slot, slot, ag_s.at[2, k], ag_r.at[2, k], sib)

    def go_a(k):
        for j in ZORDER:
            z1(k, j).start()

    def go_b(k):
        z1(k).wait_recv()
        for j in YORDER:
            y2(k, j).start()

    def go_c(k):
        y2(k).wait_recv()
        c_send(k).start()

    def left(k):
        for copies in (y2(k), z1(k), c_send(k)):
            copies.wait_send()

    def encode(k, carry):
        head = carry is None
        load_tok(k).wait()
        x = tok[pl.ds(k * CN, CN)].reshape(ROWS, D)
        acc = x.astype(F32)
        for j in range(NFB):
            if head:
                load_in(j).wait()
                load_out(j).wait()
            h = jnp.dot(x, win[:, j * FB:(j + 1) * FB], preferred_element_type=F32)
            a = (h * 0.5 * (1.0 + lax.erf(h * 0.7071067811865476))).astype(BF)
            acc = acc + jnp.dot(a, wout[j * FB:(j + 1) * FB, :], preferred_element_type=F32)
            if j == 1 and head:
                meet()
            if j == 2 and not head:
                @pl.when(k >= 2)
                def _():
                    go_b(k - 2)
        cent = acc - jnp.mean(acc, axis=1, keepdims=True)
        var = jnp.mean(cent * cent, axis=1, keepdims=True)
        norm = cent * lax.rsqrt(var + EPS)
        emb[z, y, c, k] = jnp.mean(norm.reshape(CN, TOK, D), axis=1).astype(BF)

        go_a(k)
        return carry

    encode(0, None)
    lax.fori_loop(1, CHUNKS, encode, 0)
    for n in range(2):
        w_recv(n).wait_recv()
        w_fwd(n).start()
    go_b(2)

    load_tiles().wait()
    id_all().wait_recv()
    tile_all().wait_recv()
    for n in range(QUAD):
        spread[pl.ds(n * TILES * SUB, TILES * SUB), :] = tiles[n].astype(F32).reshape(TILES * SUB, BLK)
    cell = jnp.maximum(jnp.max(ids[...], axis=0), ids_out[0])[0:1, :]
    pick = (lax.broadcasted_iota(jnp.int32, (BLOCKS * BLOCKS, QUAD * TILES), 0) == cell).astype(BF)
    dlane = lax.broadcasted_iota(jnp.int32, (BLOCKS, BLK), 1)

    def place(n, found):
        for u in range(UNROLL):
            i = n * UNROLL + u
            rows = spread[pl.ds(i, QUAD * TILES, stride=SUB), :].astype(BF)
            got = jnp.dot(pick, rows, preferred_element_type=F32)
            total = got[:BLOCKS]
            to = pl.ds(pl.multiple_of(i * BLOCKS, BLOCKS), BLOCKS)
            for s in range(BLOCKS):
                part = got[s * BLOCKS:(s + 1) * BLOCKS]
                if s:
                    total = total + part
                adj[to, s * BLK:(s + 1) * BLK] = part.astype(BF)
            found = found + jnp.where(dlane == i, jnp.sum(total, axis=1, keepdims=True), 0.0)
        return found

    deg[...] = lax.fori_loop(0, SUB // UNROLL, place, jnp.zeros((BLOCKS, BLK), F32))

    partner = at(z, yoff(2), c)
    d_first = remote(deg, deg_in, d_s.at[0], d_r.at[0], partner)
    d_first.start()
    go_b(3)
    for n in range(2):
        w_fwd_recv(n).wait_recv()
    for n in range(1, 4):
        w_sib(n).start()
    total_rows = BLOCKS * SUB
    r = lax.broadcasted_iota(jnp.int32, (total_rows, total_rows), 0)
    col = lax.broadcasted_iota(jnp.int32, (total_rows, total_rows), 1)
    turn = (col == lax.rem(r, SUB) * BLOCKS + r // SUB).astype(BF)
    for n in range(4):
        cols = slice(n * 512, (n + 1) * 512)
        adj_t[:, cols] = jnp.dot(turn, adj[:, cols], preferred_element_type=F32).astype(BF)
    go_c(0)
    go_c(1)
    emb_v[...] = emb[z, y, c].astype(F32).reshape(NODES, D).astype(BF)
    save_emb = pltpu.make_async_copy(emb_v, emb_out, load_sem.at[15])
    save_emb.start()
    go_c(2)
    d_first.wait_recv()
    deg_sum[...] = deg[...] + deg_in[...]

    def d_send(j):
        return remote(deg_sum, deg_all.at[j], d_s.at[1], d_r.at[1], at(zoff(j), y, c))

    def d_all():
        slot = deg_all.at[pl.ds(1, NZ - 1)]
        return remote(slot, slot, d_s.at[1], d_r.at[1], sib)

    for j in range(1, NZ):
        d_send(j).start()

    go_c(3)
    for k in range(CHUNKS):
        c_recv(k).wait_recv()

    def vy(f):
        if f:
            src, dst = out_y.at[f, :, 1 - yh], in_y.at[f]
        else:
            src, dst = out_p, in_p
        return remote(src, dst, vy_s.at[f], vy_r.at[f], partner)

    def vz(f, j):
        if f:
            src, dst = out_z.at[f, zoff(j)], in_z.at[f, j]
        else:
            src, dst = out_y.at[0, zoff(j)], in_z0.at[j]
        return remote(src, dst, vz_s.at[f], vz_r.at[f], at(zoff(j), y, c))

    def vz_all(f):
        slot = in_z.at[f, pl.ds(1, NZ - 1)] if f else in_z0.at[pl.ds(1, NZ - 1)]
        return remote(slot, slot, vz_s.at[f], vz_r.at[f], sib)

    def go_vz(f):
        vy(f).wait_recv()
        both = own[f, :, yh] + in_y[f].astype(F32)
        own[f, :, yh] = both
        out_z[f] = both.astype(BF)
        for j in ZORDER:
            vz(f, j).start()

    for f in range(NFC):
        e = emb[:, :, :, :, :, f * FC:(f + 1) * FC].astype(F32).reshape(NZ * NY * NC * NODES, FC).astype(BF)
        v = jnp.dot(adj_t[...], e, preferred_element_type=F32).reshape(NZ, 2, SUB, FC)
        own[f] = v
        out_y[f] = v.astype(BF)
        if f:
            vy(f).start()
        else:
            for j in ZORDER:
                vz(0, j).start()
    id_all().wait_send()
    tile_all().wait_send()
    for n in range(2):
        w_send(n).wait_send()
        w_fwd(n).wait_send()
    for n in range(1, 4):
        w_sib(n).wait_send()

    def gone(k, carry):
        left(k)
        return carry

    lax.fori_loop(0, CHUNKS, gone, 0)
    d_first.wait_send()
    d_all().wait_send()

    for h in range(2):
        load_ws(h).wait()
    for n in range(1, 4):
        w_sib_recv(n).wait_recv()
    mine_emb = emb_v[...]
    pre = [jnp.dot(mine_emb, wg[0, n], preferred_element_type=F32) for n in range(NX)]

    go_vz(1)
    vz_all(0).wait_recv()
    for h in range(2):
        total = own[0, z, h]
        for j in range(1, NZ):
            total = total + in_z0[j, h].astype(F32)
        own[0, z, h] = total
    out_p[...] = own[0, z, 1 - yh].astype(BF)
    vy(0).start()
    go_vz(2)

    degree = deg_sum[...]
    d_all().wait_recv()
    for j in range(1, NZ):
        degree = degree + deg_all[j]
    block = g // 4
    degree = jnp.sum(
        jnp.where(lax.broadcasted_iota(jnp.int32, (BLOCKS, BLK), 0) == block, degree, 0.0), axis=0, keepdims=True
    )
    on = lax.broadcasted_iota(jnp.int32, (NODES, BLK), 0) == lax.broadcasted_iota(jnp.int32, (NODES, BLK), 1)
    column = jnp.sum(jnp.where(on, jnp.broadcast_to(degree, (NODES, BLK)), 0.0), axis=1, keepdims=True)
    scale = lax.rsqrt(1.0 + column)

    for f in range(NFC):
        total = own[f, z, yh]
        if f:
            vz_all(f).wait_recv()
            for j in range(1, NZ):
                total = total + in_z[f, j].astype(F32)
        else:
            vy(0).wait_recv()
            total = total + in_p[...].astype(F32)
        agg = (total * scale).astype(BF)
        for n in range(NX):
            pre[n] = pre[n] + jnp.dot(agg, wg[1, n, f * FC:(f + 1) * FC, :], preferred_element_type=F32)
    act = [jnp.maximum(p, 0.0) for p in pre]
    square = sum(jnp.sum(r * r, axis=1, keepdims=True) for r in act)
    inv = lax.rsqrt(square * (1.0 / HID) + EPS)
    for n in range(NX):
        node_v[:, n * 256:(n + 1) * 256] = (act[n] * inv).astype(BF)
    save_node = pltpu.make_async_copy(node_v, node_out, load_sem.at[16])
    save_node.start()

    save_emb.wait()
    save_node.wait()
    for f in range(NFC):
        vy(f).wait_send()
        vz_all(f).wait_send()


def on_device(tokens, w_in, w_out, tile_weights, tile_src, tile_dst, w_sage):
    dma = pltpu.SemaphoreType.DMA
    anywhere = pl.BlockSpec(memory_space=pl.ANY)
    smem = pl.BlockSpec(memory_space=pltpu.SMEM)
    shapes = (jax.ShapeDtypeStruct((NODES, D), BF), jax.ShapeDtypeStruct((NODES, HID), BF))
    return pl.pallas_call(
        kernel,
        out_shape=shapes,
        in_specs=[anywhere, anywhere, anywhere, anywhere, smem, smem, anywhere],
        out_specs=(anywhere, anywhere),
        scratch_shapes=[
            pltpu.VMEM((D, FF), BF),
            pltpu.VMEM((FF, D), BF),
            pltpu.VMEM((NODES, TOK, D), BF),
            pltpu.VMEM((QUAD, TILES, SUB, BLK), BF),
            pltpu.VMEM((5, 8, 128), jnp.int32),
            pltpu.VMEM((6, 8, 128), jnp.int32),
            pltpu.VMEM((QUAD * TILES * SUB, BLK), F32),
            pltpu.VMEM((BLOCKS * SUB, BLOCKS * BLK), BF),
            pltpu.VMEM((BLOCKS * SUB, BLOCKS * BLK), BF),
            pltpu.VMEM((NZ, NY, NC, CHUNKS, CN, D), BF),
            pltpu.VMEM((2, NX, D, 256), BF),
            pltpu.VMEM((NFC, NZ, 2, SUB, FC), F32),
            pltpu.VMEM((NFC, NZ, 2, SUB, FC), BF),
            pltpu.VMEM((NFC, NZ, SUB, FC), BF),
            pltpu.VMEM((NFC, NZ, SUB, FC), BF),
            pltpu.VMEM((NFC, NZ, SUB, FC), BF),
            pltpu.VMEM((NZ, 2, SUB, FC), BF),
            pltpu.VMEM((SUB, FC), BF),
            pltpu.VMEM((SUB, FC), BF),
            pltpu.VMEM((NODES, D), BF),
            pltpu.VMEM((NODES, HID), BF),
            pltpu.VMEM((BLOCKS, BLK), F32),
            pltpu.VMEM((BLOCKS, BLK), F32),
            pltpu.VMEM((BLOCKS, BLK), F32),
            pltpu.VMEM((NZ, BLOCKS, BLK), F32),
            dma((17,)),
            dma((1,)), dma((1,)),
            dma((1,)), dma((1,)),
            dma((7,)), dma((7,)),
            dma((3, CHUNKS)), dma((3, CHUNKS)),
            dma((NFC,)), dma((NFC,)),
            dma((NFC,)), dma((NFC,)),
            dma((2,)), dma((2,)),
        ],
        compiler_params=pltpu.CompilerParams(
            collective_id=0, has_side_effects=True, vmem_limit_bytes=58 * 2**20
        ),
        cost_estimate=pl.CostEstimate(flops=12_000_000_000, bytes_accessed=16_000_000, transcendentals=3_200_000),
        name="encode_and_aggregate",
    )(tokens, w_in, w_out, tile_weights, tile_src, tile_dst, w_sage)


def solution(mesh):
    return jax.shard_map(
        on_device,
        mesh=mesh,
        in_specs=(
            P(("dp", "graph"), None, None),
            P(),
            P(),
            P(("dp", "graph"), None, None),
            P(("dp", "graph")),
            P(("dp", "graph")),
            P(None, "dp"),
        ),
        out_specs=(P(("dp", "graph"), None), P(("dp", "graph"), None)),
        check_vma=False,
    )
```

time: 76.6 us -> 60.2 us (0.79)
  Pallas kernels: 72.9 us -> 56.5 us
    pallas_call x1, Pallas kernels: 72.9 us -> 56.5 us  [on_device(): pl.pallas_call(kernel, out_shape=shapes, in_specs=[anywhere, anywhere, an...]
where the time goes in v2:
time: 60.2 us; the launch traced here: 60 us
  Pallas kernels  56.5 us (94%)
  local copies, waits for them, and re-layouts  2.89 us (5%)
  between operations  0.64 us (1%)
    pallas_call x1, Pallas kernels, on_device(): pl.pallas_call(kernel, out_shape=shapes, in_specs=[anywhere, anywhere, an...  56.5 us
    unnamed x2, local copies, waits for them, and re-layouts  2.89 us

profile of v2, /device:TPU:1, one launch (start us, length us, event | category | flops | bytes accessed | tf_op | source)
XLA Modules:
  0.0 60.0 jit_solution(7188924727560591536)
XLA Ops:
  0.6 56.5 %encode_and_aggregate.1 = (bf16[32,768]{1,0:T(8,128)(2,1)}, bf16[32,1024]{1,0:T(8,128)(2,1)}) custom-call(bf16[32,32,768]{2,1,0:T(8,128)(2,1)} %tok_ref.1, bf16[768,3072]{1,0:T(8,128)(2,1)} %win_ref.1, bf16[3072,768]{1,0:T(8,128)(2,1)} %wout_ref.1, bf16[32,128,128]{2,1,0:T(8,128)(2,1)} %tw_ref.1, s32[32]{0:T(128)} %src_ref.1, s32[32]{0:T(128)} %dst_ref.1, ...), custom_call_target="tpu_custom_call" | custom-call | flops 12000000000 | bytes 16000000 | tf_op jit(solution)/shard_map/encode_and_aggregate/pallas_call | solution.py:411
  57.1 1.4 %copy.11 = bf16[32,768]{1,0:T(8,128)(2,1)} copy(bf16[32,768]{1,0:T(8,128)(2,1)} %get-tuple-element.4) | data formatting | bytes 98304
  58.6 1.5 %copy.12 = bf16[32,1024]{1,0:T(8,128)(2,1)} copy(bf16[32,1024]{1,0:T(8,128)(2,1)} %get-tuple-element.5) | data formatting | bytes 131072

commit v3 on v2

--- a/solution.py
+++ b/solution.py
@@ -23,9 +23,12 @@
 SUB = BLK // QUAD
 FC = 256
 NFC = D // FC
+PW = FC // 2
+NP = D // PW
+FIRST_Z = 1
+POLL = (0, 2, 1, 3, 4, 5)
 UNROLL = 4
 ZORDER = (4, 3, 5, 2, 6, 1, 7)
-YORDER = (2, 1, 3)
 BF, F32 = jnp.bfloat16, jnp.float32
 
 
@@ -168,17 +171,21 @@
         slot = emb.at[pl.ds(0, NZ - 1) if j is None else z, y, c, k]
         return remote(slot, slot, ag_s.at[0, k], ag_r.at[0, k], at(zoff(j or 1), y, c))
 
-    def y2(k, j=None):
-        slot = emb.at[:, pl.ds(0, NY - 1) if j is None else y, c, k]
-        return remote(slot, slot, ag_s.at[1, k], ag_r.at[1, k], at(z, yoff(j or 1), c))
+    def ya(k, n, got=False):
+        slot = emb.at[:, yoff(2 * n - 1) if got else y, c, k]
+        return remote(slot, slot, ag_s.at[1 + n, k], ag_r.at[1 + n, k], at(z, yoff(1 - 2 * n), c))
+
+    def yb(k, n, got=False):
+        slot = emb.at[pl.ds(n * (NZ // 2), NZ // 2), yoff(2 if got else 2 * n - 1), c, k]
+        return remote(slot, slot, ag_s.at[3 + n, k], ag_r.at[3 + n, k], at(z, yoff(1 - 2 * n), c))
 
     def c_send(k):
         slot = emb.at[:, :, c, k]
-        return remote(slot, slot, ag_s.at[2, k], ag_r.at[2, k], sib)
+        return remote(slot, slot, ag_s.at[5, k], ag_r.at[5, k], sib)
 
     def c_recv(k):
         slot = emb.at[:, :, 1 - c, k]
-        return remote(slot, slot, ag_s.at[2, k], ag_r.at[2, k], sib)
+        return remote(slot, slot, ag_s.at[5, k], ag_r.at[5, k], sib)
 
     def go_a(k):
         for j in ZORDER:
@@ -186,15 +193,21 @@
 
     def go_b(k):
         z1(k).wait_recv()
-        for j in YORDER:
-            y2(k, j).start()
+        for n in range(2):
+            ya(k, n).start()
+
+    def go_d(k):
+        for n in range(2):
+            ya(k, n, True).wait_recv()
+            yb(k, n).start()
 
     def go_c(k):
-        y2(k).wait_recv()
+        for n in range(2):
+            yb(k, n, True).wait_recv()
         c_send(k).start()
 
     def left(k):
-        for copies in (y2(k), z1(k), c_send(k)):
+        for copies in (z1(k), ya(k, 0), ya(k, 1), yb(k, 0), yb(k, 1), c_send(k)):
             copies.wait_send()
 
     def encode(k, carry):
@@ -211,7 +224,7 @@
             acc = acc + jnp.dot(a, wout[j * FB:(j + 1) * FB, :], preferred_element_type=F32)
             if j == 1 and head:
                 meet()
-            if j == 2 and not head:
+            if j == 1 and not head:
                 @pl.when(k >= 2)
                 def _():
                     go_b(k - 2)
@@ -228,6 +241,7 @@
     for n in range(2):
         w_recv(n).wait_recv()
         w_fwd(n).start()
+    go_d(0)
     go_b(2)
 
     load_tiles().wait()
@@ -254,16 +268,16 @@
             found = found + jnp.where(dlane == i, jnp.sum(total, axis=1, keepdims=True), 0.0)
         return found
 
-    deg[...] = lax.fori_loop(0, SUB // UNROLL, place, jnp.zeros((BLOCKS, BLK), F32))
+    steps = SUB // UNROLL
+    found = lax.fori_loop(0, steps // 2, place, jnp.zeros((BLOCKS, BLK), F32))
+    go_d(1)
+    deg[...] = lax.fori_loop(steps // 2, steps, place, found)
 
     partner = at(z, yoff(2), c)
     d_first = remote(deg, deg_in, d_s.at[0], d_r.at[0], partner)
     d_first.start()
     go_b(3)
-    for n in range(2):
-        w_fwd_recv(n).wait_recv()
-    for n in range(1, 4):
-        w_sib(n).start()
+    go_d(2)
     total_rows = BLOCKS * SUB
     r = lax.broadcasted_iota(jnp.int32, (total_rows, total_rows), 0)
     col = lax.broadcasted_iota(jnp.int32, (total_rows, total_rows), 1)
@@ -276,7 +290,12 @@
     emb_v[...] = emb[z, y, c].astype(F32).reshape(NODES, D).astype(BF)
     save_emb = pltpu.make_async_copy(emb_v, emb_out, load_sem.at[15])
     save_emb.start()
+    go_d(3)
     go_c(2)
+    for n in range(2):
+        w_fwd_recv(n).wait_recv()
+    for n in range(1, 4):
+        w_sib(n).start()
     d_first.wait_recv()
     deg_sum[...] = deg[...] + deg_in[...]
 
@@ -294,42 +313,56 @@
     for k in range(CHUNKS):
         c_recv(k).wait_recv()
 
-    def vy(f):
-        if f:
-            src, dst = out_y.at[f, :, 1 - yh], in_y.at[f]
+    def lanes(p):
+        return pl.ds(p % 2 * PW, PW)
+
+    def vy(p):
+        if p == FIRST_Z:
+            src, dst = out_p, in_p
         else:
-            src, dst = out_p, in_p
-        return remote(src, dst, vy_s.at[f], vy_r.at[f], partner)
-
-    def vz(f, j):
-        if f:
-            src, dst = out_z.at[f, zoff(j)], in_z.at[f, j]
+            src, dst = out_y.at[p // 2, :, 1 - yh, :, lanes(p)], in_y.at[p]
+        return remote(src, dst, vy_s.at[p], vy_r.at[p], partner)
+
+    def vz(p, j):
+        if p == FIRST_Z:
+            src, dst = out_y.at[p // 2, zoff(j), :, :, lanes(p)], in_z0.at[j]
         else:
-            src, dst = out_y.at[0, zoff(j)], in_z0.at[j]
-        return remote(src, dst, vz_s.at[f], vz_r.at[f], at(zoff(j), y, c))
-
-    def vz_all(f):
-        slot = in_z.at[f, pl.ds(1, NZ - 1)] if f else in_z0.at[pl.ds(1, NZ - 1)]
-        return remote(slot, slot, vz_s.at[f], vz_r.at[f], sib)
-
-    def go_vz(f):
-        vy(f).wait_recv()
-        both = own[f, :, yh] + in_y[f].astype(F32)
-        own[f, :, yh] = both
-        out_z[f] = both.astype(BF)
+            src, dst = out_z.at[p, zoff(j)], in_z.at[p, j]
+        return remote(src, dst, vz_s.at[p], vz_r.at[p], at(zoff(j), y, c))
+
+    def vz_all(p):
+        slot = in_z0.at[pl.ds(1, NZ - 1)] if p == FIRST_Z else in_z.at[p, pl.ds(1, NZ - 1)]
+        return remote(slot, slot, vz_s.at[p], vz_r.at[p], sib)
+
+    def go_vz(p):
+        if p == FIRST_Z:
+            vz_all(p).wait_recv()
+            for h in range(2):
+                total = own[p // 2, z, h, :, lanes(p)]
+                for j in range(1, NZ):
+                    total = total + in_z0[j, h].astype(F32)
+                own[p // 2, z, h, :, lanes(p)] = total
+            out_p[...] = own[p // 2, z, 1 - yh, :, lanes(p)].astype(BF)
+            vy(p).start()
+            return
+        vy(p).wait_recv()
+        both = own[p // 2, :, yh, :, lanes(p)] + in_y[p].astype(F32)
+        own[p // 2, :, yh, :, lanes(p)] = both
+        out_z[p] = both.astype(BF)
         for j in ZORDER:
-            vz(f, j).start()
+            vz(p, j).start()
 
     for f in range(NFC):
         e = emb[:, :, :, :, :, f * FC:(f + 1) * FC].astype(F32).reshape(NZ * NY * NC * NODES, FC).astype(BF)
         v = jnp.dot(adj_t[...], e, preferred_element_type=F32).reshape(NZ, 2, SUB, FC)
         own[f] = v
         out_y[f] = v.astype(BF)
-        if f:
-            vy(f).start()
-        else:
-            for j in ZORDER:
-                vz(0, j).start()
+        for p in (2 * f, 2 * f + 1):
+            if p == FIRST_Z:
+                for j in ZORDER:
+                    vz(p, j).start()
+            else:
+                vy(p).start()
     id_all().wait_send()
     tile_all().wait_send()
     for n in range(2):
@@ -353,16 +386,8 @@
     mine_emb = emb_v[...]
     pre = [jnp.dot(mine_emb, wg[0, n], preferred_element_type=F32) for n in range(NX)]
 
-    go_vz(1)
-    vz_all(0).wait_recv()
-    for h in range(2):
-        total = own[0, z, h]
-        for j in range(1, NZ):
-            total = total + in_z0[j, h].astype(F32)
-        own[0, z, h] = total
-    out_p[...] = own[0, z, 1 - yh].astype(BF)
-    vy(0).start()
-    go_vz(2)
+    for p in POLL:
+        go_vz(p)
 
     degree = deg_sum[...]
     d_all().wait_recv()
@@ -377,15 +402,18 @@
     scale = lax.rsqrt(1.0 + column)
 
     for f in range(NFC):
-        total = own[f, z, yh]
-        if f:
-            vz_all(f).wait_recv()
-            for j in range(1, NZ):
-                total = total + in_z[f, j].astype(F32)
-        else:
-            vy(0).wait_recv()
-            total = total + in_p[...].astype(F32)
-        agg = (total * scale).astype(BF)
+        sides = []
+        for p in (2 * f, 2 * f + 1):
+            total = own[f, z, yh, :, lanes(p)]
+            if p == FIRST_Z:
+                vy(p).wait_recv()
+                total = total + in_p[...].astype(F32)
+            else:
+                vz_all(p).wait_recv()
+                for j in range(1, NZ):
+                    total = total + in_z[p, j].astype(F32)
+            sides.append((total * scale).astype(BF))
+        agg = jnp.concatenate(sides, axis=1)
         for n in range(NX):
             pre[n] = pre[n] + jnp.dot(agg, wg[1, n, f * FC:(f + 1) * FC, :], preferred_element_type=F32)
     act = [jnp.maximum(p, 0.0) for p in pre]
@@ -398,9 +426,9 @@
 
     save_emb.wait()
     save_node.wait()
-    for f in range(NFC):
-        vy(f).wait_send()
-        vz_all(f).wait_send()
+    for p in range(NP):
+        vy(p).wait_send()
+        vz_all(p).wait_send()
 
 
 def on_device(tokens, w_in, w_out, tile_weights, tile_src, tile_dst, w_sage):
@@ -427,12 +455,12 @@
             pltpu.VMEM((2, NX, D, 256), BF),
             pltpu.VMEM((NFC, NZ, 2, SUB, FC), F32),
             pltpu.VMEM((NFC, NZ, 2, SUB, FC), BF),
-            pltpu.VMEM((NFC, NZ, SUB, FC), BF),
-            pltpu.VMEM((NFC, NZ, SUB, FC), BF),
-            pltpu.VMEM((NFC, NZ, SUB, FC), BF),
-            pltpu.VMEM((NZ, 2, SUB, FC), BF),
-            pltpu.VMEM((SUB, FC), BF),
-            pltpu.VMEM((SUB, FC), BF),
+            pltpu.VMEM((NP, NZ, SUB, PW), BF),
+            pltpu.VMEM((NP, NZ, SUB, PW), BF),
+            pltpu.VMEM((NP, NZ, SUB, PW), BF),
+            pltpu.VMEM((NZ, 2, SUB, PW), BF),
+            pltpu.VMEM((SUB, PW), BF),
+            pltpu.VMEM((SUB, PW), BF),
             pltpu.VMEM((NODES, D), BF),
             pltpu.VMEM((NODES, HID), BF),
             pltpu.VMEM((BLOCKS, BLK), F32),
@@ -443,9 +471,9 @@
             dma((1,)), dma((1,)),
             dma((1,)), dma((1,)),
             dma((7,)), dma((7,)),
-            dma((3, CHUNKS)), dma((3, CHUNKS)),
-            dma((NFC,)), dma((NFC,)),
-            dma((NFC,)), dma((NFC,)),
+            dma((6, CHUNKS)), dma((6, CHUNKS)),
+            dma((NP,)), dma((NP,)),
+            dma((NP,)), dma((NP,)),
             dma((2,)), dma((2,)),
         ],
         compiler_params=pltpu.CompilerParams(

time: 60.2 us -> 57.3 us (0.952)
  Pallas kernels: 56.5 us -> 53.6 us
    pallas_call x1, Pallas kernels: 56.5 us -> 53.6 us  [on_device(): pl.pallas_call(kernel, out_shape=shapes, in_specs=[anywhere, anywhere, an...]
where the time goes in v3:
time: 57.3 us; the launch traced here: 57.2 us
  Pallas kernels  53.6 us (94%)
  local copies, waits for them, and re-layouts  2.89 us (5%)
  between operations  0.64 us (1%)
    pallas_call x1, Pallas kernels, on_device(): pl.pallas_call(kernel, out_shape=shapes, in_specs=[anywhere, anywhere, an...  53.6 us
    unnamed x2, local copies, waits for them, and re-layouts  2.89 us

profile of v3, /device:TPU:1, one launch (start us, length us, event | category | flops | bytes accessed | tf_op | source)
XLA Modules:
  0.0 57.2 jit_solution(4532132801235183132)
XLA Ops:
  0.6 53.6 %encode_and_aggregate.1 = (bf16[32,768]{1,0:T(8,128)(2,1)}, bf16[32,1024]{1,0:T(8,128)(2,1)}) custom-call(bf16[32,32,768]{2,1,0:T(8,128)(2,1)} %tok_ref.1, bf16[768,3072]{1,0:T(8,128)(2,1)} %win_ref.1, bf16[3072,768]{1,0:T(8,128)(2,1)} %wout_ref.1, bf16[32,128,128]{2,1,0:T(8,128)(2,1)} %tw_ref.1, s32[32]{0:T(128)} %src_ref.1, s32[32]{0:T(128)} %dst_ref.1, ...), custom_call_target="tpu_custom_call" | custom-call | flops 12000000000 | bytes 16000000 | tf_op jit(solution)/shard_map/encode_and_aggregate/pallas_call | solution.py:439
  54.3 1.4 %copy.11 = bf16[32,768]{1,0:T(8,128)(2,1)} copy(bf16[32,768]{1,0:T(8,128)(2,1)} %get-tuple-element.4) | data formatting | bytes 98304
  55.7 1.5 %copy.12 = bf16[32,1024]{1,0:T(8,128)(2,1)} copy(bf16[32,1024]{1,0:T(8,128)(2,1)} %get-tuple-element.5) | data formatting | bytes 131072

commit v4 on v3

--- a/solution.py
+++ b/solution.py
@@ -29,6 +29,7 @@
 POLL = (0, 2, 1, 3, 4, 5)
 UNROLL = 4
 ZORDER = (4, 3, 5, 2, 6, 1, 7)
+YORDER = (2, 1, 3)
 BF, F32 = jnp.bfloat16, jnp.float32
 
 
@@ -179,6 +180,25 @@
         slot = emb.at[pl.ds(n * (NZ // 2), NZ // 2), yoff(2 if got else 2 * n - 1), c, k]
         return remote(slot, slot, ag_s.at[3 + n, k], ag_r.at[3 + n, k], at(z, yoff(1 - 2 * n), c))
 
+    end = CHUNKS - 1
+    front, back = pl.ds(0, D // 2), pl.ds(D // 2, D // 2)
+
+    def zy1(j=None):
+        slot = emb.at[pl.ds(0, NZ - 1) if j is None else z, y, c, end, :, front]
+        return remote(slot, slot, ag_s.at[0, end], ag_r.at[0, end], at(zoff(j or 1), y, c))
+
+    def zy2(j=None):
+        slot = emb.at[:, pl.ds(0, NY - 1) if j is None else y, c, end, :, front]
+        return remote(slot, slot, ag_s.at[1, end], ag_r.at[1, end], at(z, yoff(j or 1), c))
+
+    def yz1(j=None):
+        slot = emb.at[z, pl.ds(0, NY - 1) if j is None else y, c, end, :, back]
+        return remote(slot, slot, ag_s.at[2, end], ag_r.at[2, end], at(z, yoff(j or 1), c))
+
+    def yz2(j=None):
+        slot = emb.at[pl.ds(0, NZ - 1) if j is None else z, :, c, end, :, back]
+        return remote(slot, slot, ag_s.at[3, end], ag_r.at[3, end], at(zoff(j or 1), y, c))
+
     def c_send(k):
         slot = emb.at[:, :, c, k]
         return remote(slot, slot, ag_s.at[5, k], ag_r.at[5, k], sib)
@@ -187,7 +207,13 @@
         slot = emb.at[:, :, 1 - c, k]
         return remote(slot, slot, ag_s.at[5, k], ag_r.at[5, k], sib)
 
-    def go_a(k):
+    def go_a(k, last=False):
+        if last:
+            for j in YORDER:
+                yz1(j).start()
+            for j in ZORDER:
+                zy1(j).start()
+            return
         for j in ZORDER:
             z1(k, j).start()
 
@@ -201,17 +227,37 @@
             ya(k, n, True).wait_recv()
             yb(k, n).start()
 
+    def go_e():
+        yz1().wait_recv()
+        for j in ZORDER:
+            yz2(j).start()
+
+    def go_f():
+        zy1().wait_recv()
+        for j in YORDER:
+            zy2(j).start()
+
     def go_c(k):
-        for n in range(2):
-            yb(k, n, True).wait_recv()
+        if k < end:
+            for n in range(2):
+                yb(k, n, True).wait_recv()
+        else:
+            zy2().wait_recv()
+            yz2().wait_recv()
         c_send(k).start()
 
     def left(k):
-        for copies in (z1(k), ya(k, 0), ya(k, 1), yb(k, 0), yb(k, 1), c_send(k)):
-            copies.wait_send()
-
-    def encode(k, carry):
-        head = carry is None
+        if k < end:
+            z1(k).wait_send()
+            for n in range(2):
+                ya(k, n).wait_send()
+                yb(k, n).wait_send()
+        else:
+            for copies in (zy1, zy2, yz1, yz2):
+                copies().wait_send()
+        c_send(k).wait_send()
+
+    def encode(k, carry, head=False, last=False):
         load_tok(k).wait()
         x = tok[pl.ds(k * CN, CN)].reshape(ROWS, D)
         acc = x.astype(F32)
@@ -224,7 +270,9 @@
             acc = acc + jnp.dot(a, wout[j * FB:(j + 1) * FB, :], preferred_element_type=F32)
             if j == 1 and head:
                 meet()
-            if j == 1 and not head:
+            if j == 1 and last:
+                go_b(k - 2)
+            elif j == 1 and not head:
                 @pl.when(k >= 2)
                 def _():
                     go_b(k - 2)
@@ -233,11 +281,12 @@
         norm = cent * lax.rsqrt(var + EPS)
         emb[z, y, c, k] = jnp.mean(norm.reshape(CN, TOK, D), axis=1).astype(BF)
 
-        go_a(k)
+        go_a(k, last)
         return carry
 
-    encode(0, None)
-    lax.fori_loop(1, CHUNKS, encode, 0)
+    encode(0, 0, head=True)
+    lax.fori_loop(1, end, encode, 0)
+    encode(end, 0, last=True)
     for n in range(2):
         w_recv(n).wait_recv()
         w_fwd(n).start()
@@ -271,27 +320,30 @@
     steps = SUB // UNROLL
     found = lax.fori_loop(0, steps // 2, place, jnp.zeros((BLOCKS, BLK), F32))
     go_d(1)
+    go_e()
     deg[...] = lax.fori_loop(steps // 2, steps, place, found)
 
     partner = at(z, yoff(2), c)
     d_first = remote(deg, deg_in, d_s.at[0], d_r.at[0], partner)
     d_first.start()
-    go_b(3)
-    go_d(2)
-    total_rows = BLOCKS * SUB
-    r = lax.broadcasted_iota(jnp.int32, (total_rows, total_rows), 0)
-    col = lax.broadcasted_iota(jnp.int32, (total_rows, total_rows), 1)
+    go_f()
+    go_c(0)
+    wide = BLOCKS * SUB
+    r = lax.broadcasted_iota(jnp.int32, (wide, wide), 0)
+    col = lax.broadcasted_iota(jnp.int32, (wide, wide), 1)
     turn = (col == lax.rem(r, SUB) * BLOCKS + r // SUB).astype(BF)
+    place_of = lax.rem(col, BLK) // NODES * BLK + lax.rem(col, NODES) // CN * NODES + col // BLK * CN + lax.rem(col, CN)
+    turn_cols = (r == place_of).astype(BF)
     for n in range(4):
-        cols = slice(n * 512, (n + 1) * 512)
-        adj_t[:, cols] = jnp.dot(turn, adj[:, cols], preferred_element_type=F32).astype(BF)
-    go_c(0)
-    go_c(1)
+        cols = slice(n * wide, (n + 1) * wide)
+        turned = jnp.dot(turn, adj[:, cols], preferred_element_type=F32).astype(BF)
+        adj_t[:, cols] = jnp.dot(turned, turn_cols, preferred_element_type=F32).astype(BF)
+        if n == 1:
+            go_d(2)
+            go_c(1)
     emb_v[...] = emb[z, y, c].astype(F32).reshape(NODES, D).astype(BF)
     save_emb = pltpu.make_async_copy(emb_v, emb_out, load_sem.at[15])
     save_emb.start()
-    go_d(3)
-    go_c(2)
     for n in range(2):
         w_fwd_recv(n).wait_recv()
     for n in range(1, 4):
@@ -309,8 +361,24 @@
     for j in range(1, NZ):
         d_send(j).start()
 
+    def weighted(chunks, f):
+        left_side = [
+            adj_t[:, n * wide + k * BLK:n * wide + (k + 1) * BLK] for k in chunks for n in range(4)
+        ]
+        right_side = [
+            emb[:, :, :, k, :, f * FC:(f + 1) * FC].astype(F32).reshape(wide, FC).astype(BF) for k in chunks
+        ]
+        return jnp.dot(
+            jnp.concatenate(left_side, axis=1), jnp.concatenate(right_side, axis=0), preferred_element_type=F32
+        ).reshape(NZ, 2, SUB, FC)
+
+    go_c(2)
     go_c(3)
-    for k in range(CHUNKS):
+    for k in range(2):
+        c_recv(k).wait_recv()
+    for f in range(NFC):
+        own[f] = weighted((0, 1), f)
+    for k in range(2, CHUNKS):
         c_recv(k).wait_recv()
 
     def lanes(p):
@@ -353,8 +421,7 @@
             vz(p, j).start()
 
     for f in range(NFC):
-        e = emb[:, :, :, :, :, f * FC:(f + 1) * FC].astype(F32).reshape(NZ * NY * NC * NODES, FC).astype(BF)
-        v = jnp.dot(adj_t[...], e, preferred_element_type=F32).reshape(NZ, 2, SUB, FC)
+        v = own[f] + weighted((2, 3), f)
         own[f] = v
         out_y[f] = v.astype(BF)
         for p in (2 * f, 2 * f + 1):
@@ -371,11 +438,8 @@
     for n in range(1, 4):
         w_sib(n).wait_send()
 
-    def gone(k, carry):
+    for k in range(CHUNKS):
         left(k)
-        return carry
-
-    lax.fori_loop(0, CHUNKS, gone, 0)
     d_first.wait_send()
     d_all().wait_send()
 

time: 57.3 us -> 55.5 us (0.969)
  Pallas kernels: 53.6 us -> 51.7 us
    pallas_call x1, Pallas kernels: 53.6 us -> 51.7 us  [on_device(): pl.pallas_call(kernel, out_shape=shapes, in_specs=[anywhere, anywhere, an...]
where the time goes in v4:
time: 55.5 us; the launch traced here: 55.3 us
  Pallas kernels  51.7 us (93%)
  local copies, waits for them, and re-layouts  2.89 us (5%)
  between operations  0.64 us (1%)
    pallas_call x1, Pallas kernels, on_device(): pl.pallas_call(kernel, out_shape=shapes, in_specs=[anywhere, anywhere, an...  51.7 us
    unnamed x2, local copies, waits for them, and re-layouts  2.89 us

profile of v4, /device:TPU:1, one launch (start us, length us, event | category | flops | bytes accessed | tf_op | source)
XLA Modules:
  0.0 55.3 jit_solution(5557998546557697935)
XLA Ops:
  0.6 51.7 %encode_and_aggregate.1 = (bf16[32,768]{1,0:T(8,128)(2,1)}, bf16[32,1024]{1,0:T(8,128)(2,1)}) custom-call(bf16[32,32,768]{2,1,0:T(8,128)(2,1)} %tok_ref.1, bf16[768,3072]{1,0:T(8,128)(2,1)} %win_ref.1, bf16[3072,768]{1,0:T(8,128)(2,1)} %wout_ref.1, bf16[32,128,128]{2,1,0:T(8,128)(2,1)} %tw_ref.1, s32[32]{0:T(128)} %src_ref.1, s32[32]{0:T(128)} %dst_ref.1, ...), custom_call_target="tpu_custom_call" | custom-call | flops 12000000000 | bytes 16000000 | tf_op jit(solution)/shard_map/encode_and_aggregate/pallas_call | solution.py:503
  52.4 1.4 %copy.11 = bf16[32,768]{1,0:T(8,128)(2,1)} copy(bf16[32,768]{1,0:T(8,128)(2,1)} %get-tuple-element.4) | data formatting | bytes 98304
  53.8 1.5 %copy.12 = bf16[32,1024]{1,0:T(8,128)(2,1)} copy(bf16[32,1024]{1,0:T(8,128)(2,1)} %get-tuple-element.5) | data formatting | bytes 131072

commit v5 on v4

--- a/solution.py
+++ b/solution.py
@@ -27,7 +27,7 @@
 NP = D // PW
 FIRST_Z = 1
 POLL = (0, 2, 1, 3, 4, 5)
-UNROLL = 4
+UNROLL = 8
 ZORDER = (4, 3, 5, 2, 6, 1, 7)
 YORDER = (2, 1, 3)
 BF, F32 = jnp.bfloat16, jnp.float32
@@ -329,8 +329,8 @@
     go_f()
     go_c(0)
     wide = BLOCKS * SUB
-    r = lax.broadcasted_iota(jnp.int32, (wide, wide), 0)
-    col = lax.broadcasted_iota(jnp.int32, (wide, wide), 1)
+    r = lax.broadcasted_iota(jnp.int32, (wide, 1), 0)
+    col = lax.broadcasted_iota(jnp.int32, (1, wide), 1)
     turn = (col == lax.rem(r, SUB) * BLOCKS + r // SUB).astype(BF)
     place_of = lax.rem(col, BLK) // NODES * BLK + lax.rem(col, NODES) // CN * NODES + col // BLK * CN + lax.rem(col, CN)
     turn_cols = (r == place_of).astype(BF)

time: 55.5 us -> 55.9 us (level)
  no operation moved by 1% of the time
where the time goes in v5:
time: 55.9 us; the launch traced here: 55.7 us
  Pallas kernels  52.1 us (93%)
  local copies, waits for them, and re-layouts  2.89 us (5%)
  between operations  0.64 us (1%)
    pallas_call x1, Pallas kernels, on_device(): pl.pallas_call(kernel, out_shape=shapes, in_specs=[anywhere, anywhere, an...  52.1 us
    unnamed x2, local copies, waits for them, and re-layouts  2.89 us

profile of v5, /device:TPU:1, one launch (start us, length us, event | category | flops | bytes accessed | tf_op | source)
XLA Modules:
  0.0 55.7 jit_solution(17238792376051754644)
XLA Ops:
  0.6 52.1 %encode_and_aggregate.1 = (bf16[32,768]{1,0:T(8,128)(2,1)}, bf16[32,1024]{1,0:T(8,128)(2,1)}) custom-call(bf16[32,32,768]{2,1,0:T(8,128)(2,1)} %tok_ref.1, bf16[768,3072]{1,0:T(8,128)(2,1)} %win_ref.1, bf16[3072,768]{1,0:T(8,128)(2,1)} %wout_ref.1, bf16[32,128,128]{2,1,0:T(8,128)(2,1)} %tw_ref.1, s32[32]{0:T(128)} %src_ref.1, s32[32]{0:T(128)} %dst_ref.1, ...), custom_call_target="tpu_custom_call" | custom-call | flops 12000000000 | bytes 16000000 | tf_op jit(solution)/shard_map/encode_and_aggregate/pallas_call | solution.py:503
  52.8 1.4 %copy.11 = bf16[32,768]{1,0:T(8,128)(2,1)} copy(bf16[32,768]{1,0:T(8,128)(2,1)} %get-tuple-element.4) | data formatting | bytes 98304
  54.2 1.5 %copy.12 = bf16[32,1024]{1,0:T(8,128)(2,1)} copy(bf16[32,1024]{1,0:T(8,128)(2,1)} %get-tuple-element.5) | data formatting | bytes 131072
